TPU v7x, 128 devices: a whole 4x4x4 slice. The times are simulated.
128 devices in a mesh: worker: 8 (over y, x_hi), fsdp: 16 (over x_lo, z, core).
Axes of the slice: x: 4 (x_hi: 2, x_lo: 2; x = x_hi * 2 + x_lo), y: 4, z: 4, core: 2. Of those that a mesh axis runs over, the one named last changes fastest.
Arguments:
- hidden: bfloat16 [49152, 8192], P(('worker', 'fsdp')), may hold values from -6 to 6
- key_grad: bfloat16 [49152, 1024], P(('worker', 'fsdp')), may hold values from -6 to 6
- local_weight: float32 [8, 8192, 1024], P('worker', 'fsdp'), may hold values from -3 to 3
- global_weight: float32 [8192, 1024], P('fsdp'), may hold values from -3 to 3
- momentum: float32 [8192, 1024], P('fsdp'), may hold values from -3 to 3
Outputs:
- keys: bfloat16 [49152, 1024], P(('worker', 'fsdp'))
- hidden_grad: bfloat16 [49152, 8192], P(('worker', 'fsdp'))
- merged_weight: float32 [8, 8192, 1024], P('worker', 'fsdp')
- global_new: float32 [8192, 1024], P('fsdp')
- momentum_new: float32 [8192, 1024], P('fsdp')
All inputs are finite; a program needn't handle non-finite values.
Results may differ from a plain program's by a relative error of at most 0.0085.
Values may be sent and summed in bfloat16 or wider, within the bound.
A program may use at most 192 MiB of HBM per device.

v0:
```python
import jax
import jax.numpy as jnp
from jax import lax
from jax.sharding import PartitionSpec as P

D = 8192


momentum_coef = 0.9
outer_rate = 0.7
inner_rate = 0.3
mix_weight = 0.5


def outer_update(weight, global_weight, momentum):
    count = lax.axis_size("worker")
    delta = lax.psum(global_weight - weight, "worker") / count
    moment_next = momentum_coef * momentum + delta
    global_next = global_weight - outer_rate * (momentum_coef * moment_next + delta)
    return (global_next, moment_next)


def shards(hidden, key_grad, local_weight, global_weight, momentum):
    weight = local_weight[0]
    scale = D ** (-0.5)
    whole_weight = lax.all_gather(weight.astype(jnp.bfloat16), "fsdp", axis=0, tiled=True)
    keys = (jnp.dot(hidden, whole_weight, preferred_element_type=jnp.float32) * scale).astype(
        jnp.bfloat16
    )
    back = lax.dot_general(
        key_grad, whole_weight, (((1,), (1,)), ((), ())), preferred_element_type=jnp.float32
    )
    back = (back * scale).astype(jnp.bfloat16)
    product = lax.dot_general(
        hidden, key_grad, (((0,), (0,)), ((), ())), preferred_element_type=jnp.float32
    )
    grad = lax.psum_scatter(
        (product * scale).astype(jnp.bfloat16), "fsdp", scatter_dimension=0, tiled=True
    ).astype(jnp.float32)
    global_next, moment_next = outer_update(weight, global_weight, momentum)
    merged = mix_weight * (weight - inner_rate * grad) + (1.0 - mix_weight) * global_next
    return (keys, back, merged[None], global_next, moment_next)


def solution(mesh):
    placed = (
        P(("worker", "fsdp"), None),
        P(("worker", "fsdp"), None),
        P("worker", "fsdp", None),
        P("fsdp", None),
        P("fsdp", None),
    )
    return jax.shard_map(
        shards,
        mesh=mesh,
        in_specs=placed,
        out_specs=(
            P(("worker", "fsdp"), None),
            P(("worker", "fsdp"), None),
            P("worker", "fsdp", None),
            P("fsdp", None),
            P("fsdp", None),
        ),
        check_vma=False,
    )
```

profile of v0, /device:TPU:0, one launch (start us, length us, event | category | flops | bytes accessed | tf_op | source)
XLA Modules:
  0.0 294.0 jit_solution(7895581804356328276)
XLA Ops:
  8.0 0.0 copy-start
  8.0 0.0 copy-start.1
  8.0 0.0 all-gather.2.cloned.1.call-start
  8.1 2.9 bitcast_convert_fusion
  10.9 0.0 all-gather.2.cloned.1.call-update
  11.0 0.0 all-reduce.2.cloned.1.call-start
  11.0 0.0 copy-done.1
  11.0 3.5 %bitcast_subtract_fusion = f32[512,1024]{1,0:T(8,128)} fusion(f32[512,1024]{1,0:T(8,128)} %param.8, f32[1,512,1024]{2,1,0:T(8,128)S(1)} %copy-done.1), kind=kLoop, calls=%fused_computation.2 | loop fusion | flops 524288 | bytes 6291456 | tf_op jit(solution)/shard_map/sub | solution.py:17
  14.5 0.0 all-reduce.2.cloned.1.call-update
  14.5 0.0 reduce-scatter.2.cloned.1.call-start
  14.6 0.0 copy-done
  14.6 15.4 %multiply_convert_fusion = bf16[8192,1024]{1,0:T(8,128)(2,1)} fusion(bf16[384,8192]{1,0:T(8,128)(2,1)} %param.5, bf16[384,1024]{1,0:T(8,128)(2,1)S(1)} %copy-done), kind=kOutput, calls=%fused_computation | convolution fusion | flops 6459228160 | bytes 23855104 | tf_op jit(solution)/shard_map/dot_general | solution.py:34
  30.0 0.0 reduce-scatter.2.cloned.1.call-update
  30.0 109.0 %all-gather.2.cloned.1.call-done = bf16[8192,1024]{1,0:T(8,128)(2,1)} async-done(((bf16[512,1024]{1,0:T(8,128)(2,1)}), bf16[8192,1024]{1,0:T(8,128)(2,1)}) %all-gather.2.cloned.1.call-update) | async-done | bytes 16777232 | tf_op jit(solution)/shard_map/all_gather | solution.py:26
  139.0 12.1 %multiply_convert_fusion.1 = bf16[384,8192]{1,0:T(8,128)(2,1)} fusion(bf16[384,1024]{1,0:T(8,128)(2,1)S(1)} %copy-done, bf16[8192,1024]{1,0:T(8,128)(2,1)} %all-gather.2.cloned.1.call-done), kind=kOutput, calls=%fused_computation.1 | convolution fusion | flops 6448742400 | bytes 23855104 | tf_op jit(solution)/shard_map/dot_general | solution.py:30
  151.1 13.0 %fusion.3 = bf16[384,1024]{1,0:T(8,128)(2,1)} fusion(bf16[384,8192]{1,0:T(8,128)(2,1)} %param.5, bf16[8192,1024]{1,0:T(8,128)(2,1)} %all-gather.2.cloned.1.call-done), kind=kOutput, calls=%fused_computation.11 | convolution fusion | flops 6443237376 | bytes 23855104 | tf_op jit(solution)/shard_map/dot_general | solution.py:27
  164.1 70.8 %all-reduce.2.cloned.1.call-done = f32[512,1024]{1,0:T(8,128)} async-done(((f32[512,1024]{1,0:T(8,128)}), f32[512,1024]{1,0:T(8,128)}) %all-reduce.2.cloned.1.call-update) | async-done | bytes 2097168 | tf_op jit(solution)/shard_map/psum | solution.py:17
  234.9 44.4 %reduce-scatter.2.cloned.1.call-done = bf16[512,1024]{1,0:T(8,128)(2,1)} async-done(((bf16[8192,1024]{1,0:T(8,128)(2,1)}), bf16[512,1024]{1,0:T(8,128)(2,1)}) %reduce-scatter.2.cloned.1.call-update) | async-done | bytes 1048592 | tf_op jit(solution)/shard_map/reduce_scatter | solution.py:37
  279.4 7.2 %fusion.2 = (f32[1,512,1024]{2,1,0:T(8,128)}, f32[512,1024]{1,0:T(8,128)}, f32[512,1024]{1,0:T(8,128)}) fusion(f32[1,512,1024]{2,1,0:T(8,128)S(1)} %copy-done.1, bf16[512,1024]{1,0:T(8,128)(2,1)} %reduce-scatter.2.cloned.1.call-done, f32[512,1024]{1,0:T(8,128)} %param.8, f32[512,1024]{1,0:T(8,128)} %all-reduce.2.cloned.1.call-done, f32[512,1024]{1,0:T(8,128)} %param.9), kind=kLoop, calls=%fused_computation.7 | loop fusion | flops 6291456 | bytes 15728640 | tf_op jit(solution)/shard_map/broadcast_in_dim | solution.py:42
Async XLA Ops:
  8.0 6.6 %copy-start = (bf16[384,1024]{1,0:T(8,128)(2,1)S(1)}, bf16[384,1024]{1,0:T(8,128)(2,1)}, u32[]{:S(2)}) copy-start(bf16[384,1024]{1,0:T(8,128)(2,1)} %param.6) | copy-start | bytes 2359300
  8.0 3.0 %copy-start.1 = (f32[1,512,1024]{2,1,0:T(8,128)S(1)}, f32[1,512,1024]{2,1,0:T(8,128)}, u32[]{:S(2)}) copy-start(f32[1,512,1024]{2,1,0:T(8,128)} %param.7) | copy-start | bytes 6291460
  8.0 130.9 %all-gather.2.cloned.1.call-start = ((), (), s32[]{:S(2)}) async-start(), calls=%async_computation.1 | async-start | bytes 17825792 | tf_op jit(solution)/shard_map/all_gather | solution.py:26
  11.0 224.0 %all-reduce.2.cloned.1.call-start = ((), (), s32[]{:S(2)}) async-start(), calls=%async_computation.3 | async-start | bytes 4194304 | tf_op jit(solution)/shard_map/psum | solution.py:17
  14.5 264.8 %reduce-scatter.2.cloned.1.call-start = ((), (), s32[]{:S(2)}) async-start(), calls=%async_computation.2 | async-start | bytes 17825792 | tf_op jit(solution)/shard_map/reduce_scatter | solution.py:37
Sparse Core Ops, SparseCore 0:
  11.1 127.7 all-gather.1
  141.4 137.9 reduce-scatter.1
Sparse Core Ops, SparseCore 1:
  14.6 220.3 all-reduce.1
where the time goes:
time: 294 us
  waiting for transfers between devices  224 us (76%)
  matrix products  40.5 us (14%)
  between operations  15.5 us (5%)
  other arithmetic  13.5 us (5%)
    all_gather x1, waiting for transfers between devices, shards(): lax.all_gather(weight.astype(jnp.bfloat16), 'fsdp', axis=0, tiled=True)  109 us
    psum x1, waiting for transfers between devices, outer_update(): delta = lax.psum(global_weight - weight, 'worker') / count  70.8 us
    reduce_scatter x1, waiting for transfers between devices, shards(): lax.psum_scatter((product * scale).astype(jnp.bfloat16), 'fsdp', scatter_...  44.4 us
    dot_general x1, matrix products, shards(): lax.dot_general(hidden, key_grad, (((0,), (0,)), ((), ())), preferred_ele...  15.4 us
    dot_general x1, matrix products, shards(): jnp.dot(hidden, whole_weight, preferred_element_type=jnp.float32) * scale  13 us
    dot_general x1, matrix products, shards(): lax.dot_general(key_grad, whole_weight, (((1,), (1,)), ((), ())), preferr...  12.1 us
    broadcast_in_dim x1, other arithmetic, shards(): return (keys, back, merged[None], global_next, moment_next)  7.15 us
  transfers between devices with their start and end apart: 3, of which 3 were waited for; matrix products, arithmetic and copies ran while one was open for 15% of the time, Pallas kernels for 0%

commit v1 on v0

v1 whole, which is shorter than its diff:
```python
import jax
import jax.numpy as jnp
from jax import lax
from jax.experimental import pallas as pl
from jax.experimental.pallas import tpu as pltpu
from jax.sharding import PartitionSpec as P

D = 8192
KV = 1024
TOK = 384
ROWS = 512
SCALE = D ** (-0.5)
MESH = pl.DeviceIdType.MESH

momentum_coef = 0.9
outer_rate = 0.7
inner_rate = 0.3
mix_weight = 0.5

AX = 320
RX = 288
ZERO, PLUS, MINUS, FAR = 0, 1, 2, 3


def slot(dx, dz):
    return dx * 4 + dz


def kernel(
    hid, kg, loc, glo, mom,
    o_keys, o_back, o_merged, o_glob, o_mom,
    W, H, K, G, acc, acc_in, keys_st, back_st, L, GL, M, DF, RY, A, RXH, DL,
    x_zpart, x_last, half_x, half_z, full_x, full_z,
    ssem, rsem, lsem,
):
    f32, bf16 = jnp.float32, jnp.bfloat16
    w, f = lax.axis_index("worker"), lax.axis_index("fsdp")
    y, xh = w // 2, lax.rem(w, 2)
    xl, z, c = f // 8, lax.rem(f, 8) // 2, lax.rem(f, 2)

    def dev(y_, xh_, xl_, z_, c_):
        return (y_ * 2 + xh_, xl_ * 8 + z_ * 2 + c_)

    z_up, z_down = lax.rem(z + 1, 4), lax.rem(z + 3, 4)
    up, down = dev(y, xh, xl, z_up, c), dev(y, xh, xl, z_down, c)
    pair = dev(y, xh, 1 - xl, z, c)
    core = dev(y, xh, xl, z, 1 - c)
    cross = dev(y, 1 - xh, xl, z, c)
    ys = [dev(lax.rem(y + k, 4), xh, xl, z, c) for k in (1, 2, 3)]

    counts = {"remote": 0, "local": 0}
    sent = []

    def send(src, dst, to, keep=True):
        i = counts["remote"]
        counts["remote"] += 1
        copy = pltpu.make_async_remote_copy(
            src_ref=src, dst_ref=dst, send_sem=ssem.at[i], recv_sem=rsem.at[i],
            device_id=to, device_id_type=MESH,
        )
        copy.start()
        if keep:
            sent.append(copy)
        return copy

    def move(src, dst):
        i = counts["local"]
        counts["local"] += 1
        copy = pltpu.make_async_copy(src, dst, lsem.at[i])
        copy.start()
        return copy

    def columns(s, parity):
        dx, dz = divmod(s, 4)
        shift = (0, 1, 3, 2)[dz]
        chip = (xl + dx - 2 * xl * dx) * 4 + lax.rem(z + shift, 4)
        return pl.ds(pl.multiple_of((chip * 2 + parity) * ROWS, ROWS), ROWS)

    ld_loc = [move(loc.at[pl.ds(AX, ROWS - AX)], L.at[pl.ds(AX, ROWS - AX)]),
              move(loc.at[pl.ds(0, AX)], L.at[pl.ds(0, AX)])]
    ld_kg = move(kg, K.at[pl.ds(0, TOK)])
    ld_glo = move(glo, GL)
    order = [slot(1, FAR), slot(0, FAR), slot(1, PLUS), slot(1, MINUS),
             slot(0, PLUS), slot(0, MINUS), slot(1, ZERO), slot(0, ZERO)]

    barrier = pltpu.get_barrier_semaphore()
    partners = [up, down, pair, core, cross, *ys]
    for d in partners:
        pl.semaphore_signal(barrier, inc=1, device_id=d, device_id_type=MESH)
    pl.semaphore_wait(barrier, len(partners))

    def rounded(lo, n):
        @pl.loop(0, n // 32)
        def _(r):
            at = pl.ds(pl.multiple_of(lo + r * 32, 32), 32)
            W[slot(0, ZERO), at, :] = L[at, :].astype(bf16)

    aX, aZ = pl.ds(0, AX), pl.ds(AX, ROWS - AX)
    hX = (pl.ds(0, AX // 2), pl.ds(AX // 2, AX // 2))
    nz = (ROWS - AX) // 2
    hZ = (pl.ds(AX, nz), pl.ds(AX + nz, nz))
    own = slot(0, ZERO)

    def w_send(src, dst, rows, to):
        return send(W.at[src, rows], W.at[dst, rows], to)

    ld_loc[0].wait()
    rounded(AX, ROWS - AX)
    up_z = w_send(own, slot(0, MINUS), aZ, up)
    down_z = w_send(own, slot(0, PLUS), aZ, down)
    ld_loc[1].wait()
    rounded(0, AX)
    pair_x = w_send(own, slot(1, ZERO), aX, pair)
    up_x = w_send(own, slot(0, MINUS), aX, up)
    down_x = w_send(own, slot(0, PLUS), aX, down)
    pair_z = w_send(own, slot(1, ZERO), aZ, pair)

    sw_kg = send(kg, K.at[pl.ds(TOK, TOK)], core)
    sw_hid, ld_hid = {}, {}
    for s in order:
        sw_hid[s] = send(hid.at[:, columns(s, 1 - c)], H.at[s, pl.ds(TOK, TOK)], core)
        ld_hid[s] = move(hid.at[:, columns(s, c)], H.at[s, pl.ds(0, TOK)])
    ld_mom = move(mom, M)

    ld_glo.wait()

    @pl.loop(0, ROWS // 32)
    def _(r):
        at = pl.ds(pl.multiple_of(r * 32, 32), 32)
        DF[at, :] = (GL[at, :] - L[at, :]).astype(bf16)

    def quarter(q):
        return pl.ds(pl.multiple_of(q * 128, 128), 128)

    y_parts = [send(DF.at[quarter(lax.rem(y + k, 4))], RY.at[k - 1], ys[k - 1]) for k in (1, 2, 3)]

    ld_kg.wait()
    sw_kg.wait_recv()

    def product(s):
        ld_hid[s].wait()
        sw_hid[s].wait_recv()

        @pl.loop(0, KV // 256)
        def _(j):
            at = pl.ds(pl.multiple_of(j * 256, 256), 256)
            term = lax.dot_general(H[s], K[:, at], (((0,), (0,)), ((), ())), preferred_element_type=f32)
            G[s, :, at] = (term * SCALE).astype(bf16)

    state = {"first": True, "n": 0, "out": {}}

    def forward(s):
        first = state["first"]
        state["first"] = False

        @pl.loop(0, KV // 256)
        def _(j):
            at = pl.ds(pl.multiple_of(j * 256, 256), 256)
            part = jnp.dot(H[s], W[s, :, at], preferred_element_type=f32)
            if first:
                acc[:, at] = part
            else:
                acc[:, at] += part

        n = state["n"]
        state["n"] += 1
        b = n % 2
        if n >= 2:
            mine, theirs = state["out"][n - 2]
            mine.wait()
            theirs.wait_send()

        @pl.loop(0, ROWS // 256)
        def _(j):
            at = pl.ds(pl.multiple_of(j * 256, 256), 256)
            back = lax.dot_general(K[...], W[s, at, :], (((1,), (1,)), ((), ())), preferred_element_type=f32)
            back_st[b, :, at] = (back * SCALE).astype(bf16)

        cols = columns(s, c)
        mine = move(back_st.at[b, pl.ds(0, TOK)], o_back.at[:, cols])
        theirs = send(back_st.at[b, pl.ds(TOK, TOK)], o_back.at[:, cols], core, keep=False)
        state["out"][n] = (mine, theirs)

    for s in order[:6]:
        product(s)
    up_z.wait_recv()
    down_z.wait_recv()
    far_z = (w_send(slot(0, MINUS), slot(0, FAR), hZ[0], up), w_send(slot(0, PLUS), slot(0, FAR), hZ[1], down))
    pair_zm = w_send(slot(0, MINUS), slot(1, MINUS), aZ, pair)
    pair_zp = w_send(slot(0, PLUS), slot(1, PLUS), aZ, pair)
    for s in order[6:]:
        product(s)
    pair_x.wait_recv()
    up_px = w_send(slot(1, ZERO), slot(1, MINUS), aX, up)
    down_px = w_send(slot(1, ZERO), slot(1, PLUS), aX, down)
    forward(own)

    for copy in y_parts:
        copy.wait_recv()

    @pl.loop(0, 128 // 32)
    def _(r):
        at = pl.ds(pl.multiple_of(r * 32, 32), 32)
        mine = DF[pl.ds(pl.multiple_of(y * 128 + r * 32, 32), 32), :].astype(f32)
        total = (mine + RY[0, at, :].astype(f32)) + (RY[1, at, :].astype(f32) + RY[2, at, :].astype(f32))
        A[at, :] = total.astype(bf16)

    x_sum = send(A, RXH, cross)

    up_x.wait_recv()
    down_x.wait_recv()
    far_x = (w_send(slot(0, MINUS), slot(0, FAR), hX[0], up), w_send(slot(0, PLUS), slot(0, FAR), hX[1], down))
    forward(slot(0, PLUS))
    forward(slot(0, MINUS))
    for copy in far_z:
        copy.wait_recv()
    pair_z2 = w_send(slot(0, FAR), slot(1, FAR), aZ, pair)
    pair_z.wait_recv()
    forward(slot(1, ZERO))

    x_sum.wait_recv()

    @pl.loop(0, 128 // 32)
    def _(r):
        at = pl.ds(pl.multiple_of(r * 32, 32), 32)
        total = A[at, :].astype(f32) + RXH[at, :].astype(f32)
        DL[pl.ds(pl.multiple_of(y * 128 + r * 32, 32), 32), :] = (total * 0.125).astype(bf16)

    y_back = [send(DL.at[quarter(y)], DL.at[quarter(y)], ys[k - 1]) for k in (1, 2, 3)]

    up_px.wait_recv()
    down_px.wait_recv()
    far_px = (w_send(slot(1, MINUS), slot(1, FAR), hX[0], up), w_send(slot(1, PLUS), slot(1, FAR), hX[1], down))

    gX, gZ = pl.ds(0, RX), pl.ds(RX, ROWS - RX)
    gx2, gz2 = RX // 2, (ROWS - RX) // 2
    x_parts = [send(G.at[slot(1, dz), gZ], x_zpart.at[dz], pair) for dz in (FAR, PLUS, MINUS, ZERO)]
    halves = {}
    for dx in (1, 0):
        halves[dx] = (send(G.at[slot(dx, FAR), pl.ds(0, gx2)], half_x.at[dx, 0], up),
                      send(G.at[slot(dx, FAR), pl.ds(gx2, gx2)], half_x.at[dx, 1], down))

    for copy in far_x:
        copy.wait_recv()
    forward(slot(0, FAR))
    pair_zp.wait_recv()
    forward(slot(1, PLUS))
    pair_zm.wait_recv()
    forward(slot(1, MINUS))

    for copy in y_back:
        copy.wait_recv()
    ld_mom.wait()

    @pl.loop(0, ROWS // 16)
    def _(r):
        at = pl.ds(pl.multiple_of(r * 16, 16), 16)
        delta = DL[at, :].astype(f32)
        moment = momentum_coef * M[at, :] + delta
        M[at, :] = moment
        GL[at, :] = GL[at, :] - outer_rate * (momentum_coef * moment + delta)

    st_mom = move(M, o_mom)
    st_glo = move(GL, o_glob)

    def add(s, lo, n, *terms):
        @pl.loop(0, n // 16)
        def _(r):
            at = pl.ds(pl.multiple_of(lo + r * 16, 16), 16)
            rows = pl.ds(pl.multiple_of(r * 16, 16), 16)
            total = G[s, at, :].astype(f32)
            for term in terms:
                total += term[rows, :].astype(f32)
            G[s, at, :] = total.astype(bf16)

    fulls = {}

    def x_full(dx):
        halves[dx][0].wait_recv()
        add(slot(dx, PLUS), 0, gx2, half_x.at[dx, 0])
        u = send(G.at[slot(dx, PLUS), gX], full_x.at[dx, 0], up)
        halves[dx][1].wait_recv()
        add(slot(dx, MINUS), gx2, gx2, half_x.at[dx, 1])
        d = send(G.at[slot(dx, MINUS), gX], full_x.at[dx, 1], down)
        fulls[dx] = (u, d)

    for copy in far_px:
        copy.wait_recv()
    pair_z2.wait_recv()
    x_full(1)
    x_parts[0].wait_recv()
    add(slot(0, FAR), RX, ROWS - RX, x_zpart.at[FAR])
    z_halves = (send(G.at[slot(0, FAR), pl.ds(RX, gz2)], half_z.at[0], up),
                send(G.at[slot(0, FAR), pl.ds(RX + gz2, gz2)], half_z.at[1], down))
    forward(slot(1, FAR))
    keys_swap = send(acc.at[pl.ds(TOK, TOK)], acc_in, core)
    x_full(0)

    x_parts[1].wait_recv()
    x_parts[2].wait_recv()
    add(slot(0, PLUS), RX, ROWS - RX, x_zpart.at[PLUS])
    add(slot(0, MINUS), RX, ROWS - RX, x_zpart.at[MINUS])
    z_halves[0].wait_recv()
    add(slot(0, PLUS), RX, gz2, half_z.at[0])
    u = send(G.at[slot(0, PLUS), gZ], full_z.at[0], up)
    z_halves[1].wait_recv()
    add(slot(0, MINUS), RX + gz2, gz2, half_z.at[1])
    z_fulls = (u, send(G.at[slot(0, MINUS), gZ], full_z.at[1], down))

    for copy in fulls[1]:
        copy.wait_recv()
    add(slot(1, ZERO), 0, RX, full_x.at[1, 0], full_x.at[1, 1])
    last = send(G.at[slot(1, ZERO), gX], x_last, pair)

    keys_swap.wait_recv()

    @pl.loop(0, TOK // 16)
    def _(r):
        at = pl.ds(pl.multiple_of(r * 16, 16), 16)
        keys_st[at, :] = ((acc[at, :] + acc_in[at, :]) * SCALE).astype(bf16)

    st_keys = move(keys_st, o_keys)

    def merge(lo, n, *terms):
        @pl.loop(0, n // 16)
        def _(r):
            at = pl.ds(pl.multiple_of(lo + r * 16, 16), 16)
            rows = pl.ds(pl.multiple_of(r * 16, 16), 16)
            grad = G[own, at, :].astype(f32)
            for term in terms:
                grad += term[rows, :].astype(f32)
            L[at, :] = mix_weight * (L[at, :] - inner_rate * grad) + (1.0 - mix_weight) * GL[at, :]

    for copy in fulls[0]:
        copy.wait_recv()
    last.wait_recv()
    merge(0, RX, full_x.at[0, 0], full_x.at[0, 1], x_last)
    st_x = move(L.at[gX], o_merged.at[gX])
    x_parts[3].wait_recv()
    for copy in z_fulls:
        copy.wait_recv()
    merge(RX, ROWS - RX, x_zpart.at[ZERO], full_z.at[0], full_z.at[1])
    st_z = move(L.at[gZ], o_merged.at[gZ])

    for n in (6, 7):
        mine, theirs = state["out"][n]
        mine.wait()
        theirs.wait_send()
    for n in range(8):
        state["out"][n][1].wait_recv()
    for copy in sent:
        copy.wait_send()
    for copy in (st_mom, st_glo, st_keys, st_x, st_z):
        copy.wait()


def shards(hidden, key_grad, local_weight, global_weight, momentum):
    bf16, f32 = jnp.bfloat16, jnp.float32
    vm = pltpu.VMEM
    anywhere = pl.BlockSpec(memory_space=pl.ANY)
    keys, back, merged, global_next, moment_next = pl.pallas_call(
        kernel,
        out_shape=(
            jax.ShapeDtypeStruct((TOK, KV), bf16),
            jax.ShapeDtypeStruct((TOK, D), bf16),
            jax.ShapeDtypeStruct((ROWS, KV), f32),
            jax.ShapeDtypeStruct((ROWS, KV), f32),
            jax.ShapeDtypeStruct((ROWS, KV), f32),
        ),
        in_specs=[anywhere] * 5,
        out_specs=[anywhere] * 5,
        scratch_shapes=[
            vm((8, ROWS, KV), bf16),
            vm((8, 2 * TOK, ROWS), bf16),
            vm((2 * TOK, KV), bf16),
            vm((8, ROWS, KV), bf16),
            vm((2 * TOK, KV), f32),
            vm((TOK, KV), f32),
            vm((TOK, KV), bf16),
            vm((2, 2 * TOK, ROWS), bf16),
            vm((ROWS, KV), f32),
            vm((ROWS, KV), f32),
            vm((ROWS, KV), f32),
            vm((ROWS, KV), bf16),
            vm((3, 128, KV), bf16),
            vm((128, KV), bf16),
            vm((128, KV), bf16),
            vm((ROWS, KV), bf16),
            vm((4, ROWS - RX, KV), bf16),
            vm((RX, KV), bf16),
            vm((2, 2, RX // 2, KV), bf16),
            vm((2, (ROWS - RX) // 2, KV), bf16),
            vm((2, 2, RX, KV), bf16),
            vm((2, ROWS - RX, KV), bf16),
            pltpu.SemaphoreType.DMA((64,)),
            pltpu.SemaphoreType.DMA((64,)),
            pltpu.SemaphoreType.DMA((32,)),
        ],
        compiler_params=pltpu.CompilerParams(
            collective_id=0, has_side_effects=True, vmem_limit_bytes=60 * 2**20
        ),
        cost_estimate=pl.CostEstimate(flops=3 * 2 * TOK * D * KV, bytes_accessed=26 * 2**20, transcendentals=0),
        name="step",
    )(hidden, key_grad, local_weight[0], global_weight, momentum)
    return (keys, back, merged[None], global_next, moment_next)


def solution(mesh):
    placed = (
        P(("worker", "fsdp"), None),
        P(("worker", "fsdp"), None),
        P("worker", "fsdp", None),
        P("fsdp", None),
        P("fsdp", None),
    )
    return jax.shard_map(
        shards,
        mesh=mesh,
        in_specs=placed,
        out_specs=(
            P(("worker", "fsdp"), None),
            P(("worker", "fsdp"), None),
            P("worker", "fsdp", None),
            P("fsdp", None),
            P("fsdp", None),
        ),
        check_vma=False,
    )
```

time: 294 us -> 134 us (0.46)
  waiting for transfers between devices: 224 us -> 0 us
  Pallas kernels: 0 us -> 118 us
  matrix products: 40.5 us -> 0 us
  between operations: 15.5 us -> 0.65 us
  local copies, waits for them, and re-layouts: 0.01 us -> 14.4 us
  other arithmetic: 13.5 us -> 0 us
    pallas_call x0 -> x1, Pallas kernels: none -> 118 us  [shards(): pl.pallas_call(kernel, out_shape=(jax.ShapeDtypeStruct((TOK, KV), bf16),...]
    all_gather x1 -> x0, waiting for transfers between devices: 109 us -> none  [shards(): lax.all_gather(weight.astype(jnp.bfloat16), 'fsdp', axis=0, tiled=True)]
    psum x1 -> x0, waiting for transfers between devices: 70.8 us -> none  [outer_update(): delta = lax.psum(global_weight - weight, 'worker') / count]
    reduce_scatter x1 -> x0, waiting for transfers between devices: 44.4 us -> none  [shards(): lax.psum_scatter((product * scale).astype(jnp.bfloat16), 'fsdp', scatter_...]
    dot_general x3 -> x0, matrix products: 40.5 us -> none  [the longest x1 15.4 us: shards(): lax.dot_general(hidden, key_grad, (((0,), (0,)), ((), ())), preferred_ele...]
    unnamed x4 -> x11, local copies, waits for them, and re-layouts: 0.01 us -> 14.4 us
    broadcast_in_dim x1 -> x0, other arithmetic: 7.15 us -> none  [shards(): return (keys, back, merged[None], global_next, moment_next)]
    sub x1 -> x0, other arithmetic: 3.47 us -> none  [outer_update(): delta = lax.psum(global_weight - weight, 'worker') / count]
  transfers between devices with their start and end apart: 3 -> 0, of which waited for: 3 -> 0; matrix products, arithmetic and copies ran while one was open for 15% -> 0% of each run, Pallas kernels for 0% -> 0%
where the time goes in v1:
time: 134 us
  Pallas kernels  118 us (88%)
  local copies, waits for them, and re-layouts  14.4 us (11%)
    pallas_call x1, Pallas kernels, shards(): pl.pallas_call(kernel, out_shape=(jax.ShapeDtypeStruct((TOK, KV), bf16),...  118 us
    unnamed x11, local copies, waits for them, and re-layouts  14.4 us

profile of v1, /device:TPU:0, one launch (start us, length us, event | category | flops | bytes accessed | tf_op | source)
XLA Modules:
  0.0 133.5 jit_solution(17969622469020008363)
XLA Ops:
  0.6 118.5 %step.1 = (bf16[384,1024]{1,0:T(8,128)(2,1)}, bf16[384,8192]{1,0:T(8,128)(2,1)}, f32[512,1024]{1,0:T(8,128)}, f32[512,1024]{1,0:T(8,128)}, f32[512,1024]{1,0:T(8,128)}) custom-call(bf16[384,8192]{1,0:T(8,128)(2,1)} %hid.1, bf16[384,1024]{1,0:T(8,128)(2,1)} %kg.1, f32[512,1024]{1,0:T(8,128)} %bitcast.3, f32[512,1024]{1,0:T(8,128)} %glo.1, f32[512,1024]{1,0:T(8,128)} %mom.1), custom_call_target="tpu_custom_call" | custom-call | flops 19327352832 | bytes 27262976 | tf_op jit(solution)/shard_map/step/pallas_call | solution.py:361
  119.1 2.1 %copy.15 = bf16[384,1024]{1,0:T(8,128)(2,1)} copy(bf16[384,1024]{1,0:T(8,128)(2,1)} %get-tuple-element.20) | data formatting | bytes 1572864
  121.2 0.0 copy-start.2
  121.2 6.3 %copy.16 = bf16[384,8192]{1,0:T(8,128)(2,1)} copy(bf16[384,8192]{1,0:T(8,128)(2,1)} %get-tuple-element.21) | data formatting | bytes 12582912
  127.5 0.0 copy-done.2
  127.5 0.0 copy-start.1
  127.5 1.3 copy.17
  128.8 1.0 copy-done.1
  129.9 0.0 copy-start
  129.9 1.3 copy.18
  131.2 1.0 copy-done
  132.2 1.3 copy.19
Async XLA Ops:
  121.2 6.3 %copy-start.2 = (f32[512,1024]{1,0:T(8,128)S(1)}, f32[512,1024]{1,0:T(8,128)}, u32[]{:S(2)}) copy-start(f32[512,1024]{1,0:T(8,128)} %get-tuple-element.12) | copy-start | bytes 6291460
  127.5 2.3 %copy-start.1 = (f32[512,1024]{1,0:T(8,128)S(1)}, f32[512,1024]{1,0:T(8,128)}, u32[]{:S(2)}) copy-start(f32[512,1024]{1,0:T(8,128)} %get-tuple-element.23) | copy-start | bytes 6291460
  129.9 2.3 %copy-start = (f32[512,1024]{1,0:T(8,128)S(1)}, f32[512,1024]{1,0:T(8,128)}, u32[]{:S(2)}) copy-start(f32[512,1024]{1,0:T(8,128)} %get-tuple-element.24) | copy-start | bytes 6291460

commit v2 on v1

--- a/solution.py
+++ b/solution.py
@@ -28,9 +28,9 @@
 
 def kernel(
     hid, kg, loc, glo, mom,
-    o_keys, o_back, o_merged, o_glob, o_mom,
-    W, H, K, G, acc, acc_in, keys_st, back_st, L, GL, M, DF, RY, A, RXH, DL,
-    x_zpart, x_last, half_x, half_z, full_x, full_z,
+    o_keys, o_back, L, GL, M, g_own, x_own, x_last, full_own, full_z,
+    W, H, K, G, acc, acc_in, back_st, DF, RY, A, RXH, DL,
+    x_zpart, half_x, half_z, full_pair,
     ssem, rsem, lsem,
 ):
     f32, bf16 = jnp.float32, jnp.bfloat16
@@ -127,7 +127,7 @@
     @pl.loop(0, ROWS // 32)
     def _(r):
         at = pl.ds(pl.multiple_of(r * 32, 32), 32)
-        DF[at, :] = (GL[at, :] - L[at, :]).astype(bf16)
+        DF[at, :] = GL[at, :] - L[at, :]
 
     def quarter(q):
         return pl.ds(pl.multiple_of(q * 128, 128), 128)
@@ -145,7 +145,8 @@
         def _(j):
             at = pl.ds(pl.multiple_of(j * 256, 256), 256)
             term = lax.dot_general(H[s], K[:, at], (((0,), (0,)), ((), ())), preferred_element_type=f32)
-            G[s, :, at] = (term * SCALE).astype(bf16)
+            where = g_own if s == own else G.at[s]
+            where[:, at] = (term * SCALE).astype(bf16)
 
     state = {"first": True, "n": 0, "out": {}}
 
@@ -166,20 +167,18 @@
         state["n"] += 1
         b = n % 2
         if n >= 2:
-            mine, theirs = state["out"][n - 2]
-            mine.wait()
-            theirs.wait_send()
+            state["out"][n - 2].wait_send()
+        cols = columns(s, c)
 
         @pl.loop(0, ROWS // 256)
         def _(j):
             at = pl.ds(pl.multiple_of(j * 256, 256), 256)
             back = lax.dot_general(K[...], W[s, at, :], (((1,), (1,)), ((), ())), preferred_element_type=f32)
-            back_st[b, :, at] = (back * SCALE).astype(bf16)
-
-        cols = columns(s, c)
-        mine = move(back_st.at[b, pl.ds(0, TOK)], o_back.at[:, cols])
-        theirs = send(back_st.at[b, pl.ds(TOK, TOK)], o_back.at[:, cols], core, keep=False)
-        state["out"][n] = (mine, theirs)
+            back = (back * SCALE).astype(bf16)
+            o_back[:, pl.ds(pl.multiple_of(cols.start + j * 256, 256), 256)] = back[:TOK]
+            back_st[b, :, at] = back[TOK:]
+
+        state["out"][n] = send(back_st.at[b], o_back.at[:, cols], core, keep=False)
 
     for s in order[:6]:
         product(s)
@@ -201,8 +200,8 @@
     @pl.loop(0, 128 // 32)
     def _(r):
         at = pl.ds(pl.multiple_of(r * 32, 32), 32)
-        mine = DF[pl.ds(pl.multiple_of(y * 128 + r * 32, 32), 32), :].astype(f32)
-        total = (mine + RY[0, at, :].astype(f32)) + (RY[1, at, :].astype(f32) + RY[2, at, :].astype(f32))
+        mine = DF[pl.ds(pl.multiple_of(y * 128 + r * 32, 32), 32), :]
+        total = (mine + RY[0, at, :]) + (RY[1, at, :] + RY[2, at, :])
         A[at, :] = total.astype(bf16)
 
     x_sum = send(A, RXH, cross)
@@ -224,7 +223,7 @@
     def _(r):
         at = pl.ds(pl.multiple_of(r * 32, 32), 32)
         total = A[at, :].astype(f32) + RXH[at, :].astype(f32)
-        DL[pl.ds(pl.multiple_of(y * 128 + r * 32, 32), 32), :] = (total * 0.125).astype(bf16)
+        DL[pl.ds(pl.multiple_of(y * 128 + r * 32, 32), 32), :] = total * 0.125
 
     y_back = [send(DL.at[quarter(y)], DL.at[quarter(y)], ys[k - 1]) for k in (1, 2, 3)]
 
@@ -234,7 +233,8 @@
 
     gX, gZ = pl.ds(0, RX), pl.ds(RX, ROWS - RX)
     gx2, gz2 = RX // 2, (ROWS - RX) // 2
-    x_parts = [send(G.at[slot(1, dz), gZ], x_zpart.at[dz], pair) for dz in (FAR, PLUS, MINUS, ZERO)]
+    x_parts = [send(G.at[slot(1, dz), gZ], x_own if dz == ZERO else x_zpart.at[dz - 1], pair)
+               for dz in (FAR, PLUS, MINUS, ZERO)]
     halves = {}
     for dx in (1, 0):
         halves[dx] = (send(G.at[slot(dx, FAR), pl.ds(0, gx2)], half_x.at[dx, 0], up),
@@ -255,13 +255,10 @@
     @pl.loop(0, ROWS // 16)
     def _(r):
         at = pl.ds(pl.multiple_of(r * 16, 16), 16)
-        delta = DL[at, :].astype(f32)
+        delta = DL[at, :]
         moment = momentum_coef * M[at, :] + delta
         M[at, :] = moment
         GL[at, :] = GL[at, :] - outer_rate * (momentum_coef * moment + delta)
-
-    st_mom = move(M, o_mom)
-    st_glo = move(GL, o_glob)
 
     def add(s, lo, n, *terms):
         @pl.loop(0, n // 16)
@@ -278,10 +275,11 @@
     def x_full(dx):
         halves[dx][0].wait_recv()
         add(slot(dx, PLUS), 0, gx2, half_x.at[dx, 0])
-        u = send(G.at[slot(dx, PLUS), gX], full_x.at[dx, 0], up)
+        full = full_pair if dx else full_own
+        u = send(G.at[slot(dx, PLUS), gX], full.at[0], up)
         halves[dx][1].wait_recv()
         add(slot(dx, MINUS), gx2, gx2, half_x.at[dx, 1])
-        d = send(G.at[slot(dx, MINUS), gX], full_x.at[dx, 1], down)
+        d = send(G.at[slot(dx, MINUS), gX], full.at[1], down)
         fulls[dx] = (u, d)
 
     for copy in far_px:
@@ -289,7 +287,7 @@
     pair_z2.wait_recv()
     x_full(1)
     x_parts[0].wait_recv()
-    add(slot(0, FAR), RX, ROWS - RX, x_zpart.at[FAR])
+    add(slot(0, FAR), RX, ROWS - RX, x_zpart.at[FAR - 1])
     z_halves = (send(G.at[slot(0, FAR), pl.ds(RX, gz2)], half_z.at[0], up),
                 send(G.at[slot(0, FAR), pl.ds(RX + gz2, gz2)], half_z.at[1], down))
     forward(slot(1, FAR))
@@ -298,8 +296,8 @@
 
     x_parts[1].wait_recv()
     x_parts[2].wait_recv()
-    add(slot(0, PLUS), RX, ROWS - RX, x_zpart.at[PLUS])
-    add(slot(0, MINUS), RX, ROWS - RX, x_zpart.at[MINUS])
+    add(slot(0, PLUS), RX, ROWS - RX, x_zpart.at[PLUS - 1])
+    add(slot(0, MINUS), RX, ROWS - RX, x_zpart.at[MINUS - 1])
     z_halves[0].wait_recv()
     add(slot(0, PLUS), RX, gz2, half_z.at[0])
     u = send(G.at[slot(0, PLUS), gZ], full_z.at[0], up)
@@ -309,7 +307,7 @@
 
     for copy in fulls[1]:
         copy.wait_recv()
-    add(slot(1, ZERO), 0, RX, full_x.at[1, 0], full_x.at[1, 1])
+    add(slot(1, ZERO), 0, RX, full_pair.at[0], full_pair.at[1])
     last = send(G.at[slot(1, ZERO), gX], x_last, pair)
 
     keys_swap.wait_recv()
@@ -317,40 +315,53 @@
     @pl.loop(0, TOK // 16)
     def _(r):
         at = pl.ds(pl.multiple_of(r * 16, 16), 16)
-        keys_st[at, :] = ((acc[at, :] + acc_in[at, :]) * SCALE).astype(bf16)
-
-    st_keys = move(keys_st, o_keys)
+        o_keys[at, :] = ((acc[at, :] + acc_in[at, :]) * SCALE).astype(bf16)
+
+    for copy in fulls[0]:
+        copy.wait_recv()
+    last.wait_recv()
+    x_parts[3].wait_recv()
+    for copy in z_fulls:
+        copy.wait_recv()
+    for n in (6, 7):
+        state["out"][n].wait_send()
+    for n in range(8):
+        state["out"][n].wait_recv()
+    for copy in sent:
+        copy.wait_send()
+
+
+def finish(
+    keys, back, L, GL, M, g_own, x_own, x_last, full_own, full_z,
+    o_keys, o_back, o_merged, o_glob, o_mom, merged, sem,
+):
+    f32 = jnp.float32
+    copies = []
+
+    def move(src, dst):
+        copy = pltpu.make_async_copy(src, dst, sem.at[len(copies)])
+        copy.start()
+        copies.append(copy)
 
     def merge(lo, n, *terms):
         @pl.loop(0, n // 16)
         def _(r):
             at = pl.ds(pl.multiple_of(lo + r * 16, 16), 16)
             rows = pl.ds(pl.multiple_of(r * 16, 16), 16)
-            grad = G[own, at, :].astype(f32)
+            grad = g_own[at, :].astype(f32)
             for term in terms:
                 grad += term[rows, :].astype(f32)
-            L[at, :] = mix_weight * (L[at, :] - inner_rate * grad) + (1.0 - mix_weight) * GL[at, :]
-
-    for copy in fulls[0]:
-        copy.wait_recv()
-    last.wait_recv()
-    merge(0, RX, full_x.at[0, 0], full_x.at[0, 1], x_last)
-    st_x = move(L.at[gX], o_merged.at[gX])
-    x_parts[3].wait_recv()
-    for copy in z_fulls:
-        copy.wait_recv()
-    merge(RX, ROWS - RX, x_zpart.at[ZERO], full_z.at[0], full_z.at[1])
-    st_z = move(L.at[gZ], o_merged.at[gZ])
-
-    for n in (6, 7):
-        mine, theirs = state["out"][n]
-        mine.wait()
-        theirs.wait_send()
-    for n in range(8):
-        state["out"][n][1].wait_recv()
-    for copy in sent:
-        copy.wait_send()
-    for copy in (st_mom, st_glo, st_keys, st_x, st_z):
+            merged[at, :] = mix_weight * (L[at, :] - inner_rate * grad) + (1.0 - mix_weight) * GL[at, :]
+
+        move(merged.at[pl.ds(lo, n)], o_merged.at[pl.ds(lo, n)])
+
+    move(back, o_back)
+    move(M, o_mom)
+    move(GL, o_glob)
+    move(keys, o_keys)
+    merge(0, RX, full_own.at[0], full_own.at[1], x_last)
+    merge(RX, ROWS - RX, x_own, full_z.at[0], full_z.at[1])
+    for copy in copies:
         copy.wait()
 
 
@@ -358,8 +369,54 @@
     bf16, f32 = jnp.bfloat16, jnp.float32
     vm = pltpu.VMEM
     anywhere = pl.BlockSpec(memory_space=pl.ANY)
+    inside = pl.BlockSpec(memory_space=pltpu.VMEM)
+    held = [
+        vm((TOK, KV), bf16),
+        vm((TOK, D), bf16),
+        vm((ROWS, KV), f32),
+        vm((ROWS, KV), f32),
+        vm((ROWS, KV), f32),
+        vm((ROWS, KV), bf16),
+        vm((ROWS - RX, KV), bf16),
+        vm((RX, KV), bf16),
+        vm((2, RX, KV), bf16),
+        vm((2, ROWS - RX, KV), bf16),
+    ]
+    parts = pl.pallas_call(
+        kernel,
+        out_shape=held,
+        in_specs=[anywhere] * 5,
+        out_specs=[inside] * len(held),
+        scratch_shapes=[
+            vm((8, ROWS, KV), bf16),
+            vm((8, 2 * TOK, ROWS), bf16),
+            vm((2 * TOK, KV), bf16),
+            vm((8, ROWS, KV), bf16),
+            vm((2 * TOK, KV), f32),
+            vm((TOK, KV), f32),
+            vm((2, TOK, ROWS), bf16),
+            vm((ROWS, KV), f32),
+            vm((3, 128, KV), f32),
+            vm((128, KV), bf16),
+            vm((128, KV), bf16),
+            vm((ROWS, KV), f32),
+            vm((3, ROWS - RX, KV), bf16),
+            vm((2, 2, RX // 2, KV), bf16),
+            vm((2, (ROWS - RX) // 2, KV), bf16),
+            vm((2, RX, KV), bf16),
+            pltpu.SemaphoreType.DMA((64,)),
+            pltpu.SemaphoreType.DMA((64,)),
+            pltpu.SemaphoreType.DMA((32,)),
+        ],
+        compiler_params=pltpu.CompilerParams(
+            collective_id=0, has_side_effects=True, vmem_limit_bytes=44 * 2**20
+        ),
+        cost_estimate=pl.CostEstimate(flops=3 * 2 * TOK * D * KV, bytes_accessed=26 * 2**20, transcendentals=0),
+        name="step",
+    )(hidden, key_grad, local_weight[0], global_weight, momentum)
+    parts = [pltpu.with_memory_space_constraint(a, pltpu.VMEM) for a in parts]
     keys, back, merged, global_next, moment_next = pl.pallas_call(
-        kernel,
+        finish,
         out_shape=(
             jax.ShapeDtypeStruct((TOK, KV), bf16),
             jax.ShapeDtypeStruct((TOK, D), bf16),
@@ -367,41 +424,12 @@
             jax.ShapeDtypeStruct((ROWS, KV), f32),
             jax.ShapeDtypeStruct((ROWS, KV), f32),
         ),
-        in_specs=[anywhere] * 5,
+        in_specs=[inside] * len(held),
         out_specs=[anywhere] * 5,
-        scratch_shapes=[
-            vm((8, ROWS, KV), bf16),
-            vm((8, 2 * TOK, ROWS), bf16),
-            vm((2 * TOK, KV), bf16),
-            vm((8, ROWS, KV), bf16),
-            vm((2 * TOK, KV), f32),
-            vm((TOK, KV), f32),
-            vm((TOK, KV), bf16),
-            vm((2, 2 * TOK, ROWS), bf16),
-            vm((ROWS, KV), f32),
-            vm((ROWS, KV), f32),
-            vm((ROWS, KV), f32),
-            vm((ROWS, KV), bf16),
-            vm((3, 128, KV), bf16),
-            vm((128, KV), bf16),
-            vm((128, KV), bf16),
-            vm((ROWS, KV), bf16),
-            vm((4, ROWS - RX, KV), bf16),
-            vm((RX, KV), bf16),
-            vm((2, 2, RX // 2, KV), bf16),
-            vm((2, (ROWS - RX) // 2, KV), bf16),
-            vm((2, 2, RX, KV), bf16),
-            vm((2, ROWS - RX, KV), bf16),
-            pltpu.SemaphoreType.DMA((64,)),
-            pltpu.SemaphoreType.DMA((64,)),
-            pltpu.SemaphoreType.DMA((32,)),
-        ],
-        compiler_params=pltpu.CompilerParams(
-            collective_id=0, has_side_effects=True, vmem_limit_bytes=60 * 2**20
-        ),
-        cost_estimate=pl.CostEstimate(flops=3 * 2 * TOK * D * KV, bytes_accessed=26 * 2**20, transcendentals=0),
-        name="step",
-    )(hidden, key_grad, local_weight[0], global_weight, momentum)
+        scratch_shapes=[vm((ROWS, KV), f32), pltpu.SemaphoreType.DMA((8,))],
+        compiler_params=pltpu.CompilerParams(vmem_limit_bytes=8 * 2**20),
+        name="finish",
+    )(*parts)
     return (keys, back, merged[None], global_next, moment_next)
 
 

time: 134 us -> 127 us (0.948)
  local copies, waits for them, and re-layouts: 14.4 us -> 0 us
  Pallas kernels: 118 us -> 126 us
    unnamed x11 -> x0, local copies, waits for them, and re-layouts: 14.4 us -> none
    pallas_call x1 -> x2, Pallas kernels: 118 us -> 126 us  [the longest x1 121 us: shards(): pl.pallas_call(kernel, out_shape=held, in_specs=[anywhere] * 5, out_specs...]
where the time goes in v2:
time: 127 us
  Pallas kernels  126 us (99%)
    pallas_call x1, Pallas kernels, shards(): pl.pallas_call(kernel, out_shape=held, in_specs=[anywhere] * 5, out_specs...  121 us
    pallas_call x1, Pallas kernels, shards(): pl.pallas_call(finish, out_shape=(jax.ShapeDtypeStruct((TOK, KV), bf16),...  4.92 us

profile of v2, /device:TPU:0, one launch (start us, length us, event | category | flops | bytes accessed | tf_op | source)
XLA Modules:
  0.0 127.0 jit_solution(7819515975399625073)
XLA Ops:
  0.6 121.4 %step.1 = (bf16[384,1024]{1,0:T(8,128)(2,1)S(1)}, bf16[384,8192]{1,0:T(8,128)(2,1)S(1)}, f32[512,1024]{1,0:T(8,128)S(1)}, f32[512,1024]{1,0:T(8,128)S(1)}, f32[5...) custom-call(bf16[384,8192]{1,0:T(8,128)(2,1)} %hid.1, ...), custom_call_target="tpu_custom_call" | custom-call | flops 19327352832 | bytes 27262976 | tf_op jit(solution)/shard_map/step/pallas_call | solution.py:385
  122.1 4.9 %finish.1 = (bf16[384,1024]{1,0:T(8,128)(2,1)}, bf16[384,8192]{1,0:T(8,128)(2,1)}, f32[512,1024]{1,0:T(8,128)}, f32[512,1024]{1,0:T(8,128)}, f32[512,1024]{1,0:T(8,128)}) custom-call(bf16[384,1024]{1,0:T(8,128)(2,1)S(1)} %get-tuple-element.20.keys, bf16[384,8192]{1,0:T(8,128)(2,1)S(1)} %get-tuple-element.21.back, f32[512,1024]{1,0:T(8,128)S(1)} %get-tuple-element.22.L, ...), custom_call_target="tpu_custom_call" | custom-call | tf_op jit(solution)/shard_map/finish/pallas_call | solution.py:418

commit v3 on v2

--- a/solution.py
+++ b/solution.py
@@ -17,7 +17,7 @@
 inner_rate = 0.3
 mix_weight = 0.5
 
-AX = 320
+AX = 304
 RX = 288
 ZERO, PLUS, MINUS, FAR = 0, 1, 2, 3
 
@@ -90,15 +90,17 @@
     pl.semaphore_wait(barrier, len(partners))
 
     def rounded(lo, n):
-        @pl.loop(0, n // 32)
+        @pl.loop(0, n // 16)
         def _(r):
-            at = pl.ds(pl.multiple_of(lo + r * 32, 32), 32)
+            at = pl.ds(pl.multiple_of(lo + r * 16, 16), 16)
             W[slot(0, ZERO), at, :] = L[at, :].astype(bf16)
 
     aX, aZ = pl.ds(0, AX), pl.ds(AX, ROWS - AX)
-    hX = (pl.ds(0, AX // 2), pl.ds(AX // 2, AX // 2))
-    nz = (ROWS - AX) // 2
-    hZ = (pl.ds(AX, nz), pl.ds(AX + nz, nz))
+    ax2 = (AX // 32) * 16
+    hX = (pl.ds(0, ax2), pl.ds(ax2, AX - ax2))
+    hPX = (pl.ds(0, AX - ax2), pl.ds(AX - ax2, ax2))
+    az2 = (ROWS - AX) // 32 * 16
+    hZ = (pl.ds(AX, az2), pl.ds(AX + az2, ROWS - AX - az2))
     own = slot(0, ZERO)
 
     def w_send(src, dst, rows, to):
@@ -194,6 +196,9 @@
     down_px = w_send(slot(1, ZERO), slot(1, PLUS), aX, down)
     forward(own)
 
+    up_x.wait_recv()
+    down_x.wait_recv()
+    far_x = (w_send(slot(0, MINUS), slot(0, FAR), hX[0], up), w_send(slot(0, PLUS), slot(0, FAR), hX[1], down))
     for copy in y_parts:
         copy.wait_recv()
 
@@ -206,9 +211,6 @@
 
     x_sum = send(A, RXH, cross)
 
-    up_x.wait_recv()
-    down_x.wait_recv()
-    far_x = (w_send(slot(0, MINUS), slot(0, FAR), hX[0], up), w_send(slot(0, PLUS), slot(0, FAR), hX[1], down))
     forward(slot(0, PLUS))
     forward(slot(0, MINUS))
     for copy in far_z:
@@ -217,19 +219,9 @@
     pair_z.wait_recv()
     forward(slot(1, ZERO))
 
-    x_sum.wait_recv()
-
-    @pl.loop(0, 128 // 32)
-    def _(r):
-        at = pl.ds(pl.multiple_of(r * 32, 32), 32)
-        total = A[at, :].astype(f32) + RXH[at, :].astype(f32)
-        DL[pl.ds(pl.multiple_of(y * 128 + r * 32, 32), 32), :] = total * 0.125
-
-    y_back = [send(DL.at[quarter(y)], DL.at[quarter(y)], ys[k - 1]) for k in (1, 2, 3)]
-
     up_px.wait_recv()
     down_px.wait_recv()
-    far_px = (w_send(slot(1, MINUS), slot(1, FAR), hX[0], up), w_send(slot(1, PLUS), slot(1, FAR), hX[1], down))
+    far_px = (w_send(slot(1, MINUS), slot(1, FAR), hPX[0], up), w_send(slot(1, PLUS), slot(1, FAR), hPX[1], down))
 
     gX, gZ = pl.ds(0, RX), pl.ds(RX, ROWS - RX)
     gx2, gz2 = RX // 2, (ROWS - RX) // 2
@@ -239,26 +231,6 @@
     for dx in (1, 0):
         halves[dx] = (send(G.at[slot(dx, FAR), pl.ds(0, gx2)], half_x.at[dx, 0], up),
                       send(G.at[slot(dx, FAR), pl.ds(gx2, gx2)], half_x.at[dx, 1], down))
-
-    for copy in far_x:
-        copy.wait_recv()
-    forward(slot(0, FAR))
-    pair_zp.wait_recv()
-    forward(slot(1, PLUS))
-    pair_zm.wait_recv()
-    forward(slot(1, MINUS))
-
-    for copy in y_back:
-        copy.wait_recv()
-    ld_mom.wait()
-
-    @pl.loop(0, ROWS // 16)
-    def _(r):
-        at = pl.ds(pl.multiple_of(r * 16, 16), 16)
-        delta = DL[at, :]
-        moment = momentum_coef * M[at, :] + delta
-        M[at, :] = moment
-        GL[at, :] = GL[at, :] - outer_rate * (momentum_coef * moment + delta)
 
     def add(s, lo, n, *terms):
         @pl.loop(0, n // 16)
@@ -282,17 +254,53 @@
         d = send(G.at[slot(dx, MINUS), gX], full.at[1], down)
         fulls[dx] = (u, d)
 
+    for copy in far_x:
+        copy.wait_recv()
+    forward(slot(0, FAR))
+    pair_zm.wait_recv()
+    forward(slot(1, MINUS))
+    x_sum.wait_recv()
+
+    @pl.loop(0, 128 // 32)
+    def _(r):
+        at = pl.ds(pl.multiple_of(r * 32, 32), 32)
+        total = A[at, :].astype(f32) + RXH[at, :].astype(f32)
+        DL[pl.ds(pl.multiple_of(y * 128 + r * 32, 32), 32), :] = total * 0.125
+
+    y_back = [send(DL.at[quarter(y)], DL.at[quarter(y)], ys[k - 1]) for k in (1, 2, 3)]
+
+    pair_zp.wait_recv()
+    forward(slot(1, PLUS))
     for copy in far_px:
         copy.wait_recv()
     pair_z2.wait_recv()
+    forward(slot(1, FAR))
+    keys_swap = send(acc.at[pl.ds(TOK, TOK)], acc_in, core)
     x_full(1)
     x_parts[0].wait_recv()
     add(slot(0, FAR), RX, ROWS - RX, x_zpart.at[FAR - 1])
     z_halves = (send(G.at[slot(0, FAR), pl.ds(RX, gz2)], half_z.at[0], up),
                 send(G.at[slot(0, FAR), pl.ds(RX + gz2, gz2)], half_z.at[1], down))
-    forward(slot(1, FAR))
-    keys_swap = send(acc.at[pl.ds(TOK, TOK)], acc_in, core)
     x_full(0)
+
+    keys_swap.wait_recv()
+
+    @pl.loop(0, TOK // 16)
+    def _(r):
+        at = pl.ds(pl.multiple_of(r * 16, 16), 16)
+        o_keys[at, :] = ((acc[at, :] + acc_in[at, :]) * SCALE).astype(bf16)
+
+    for copy in y_back:
+        copy.wait_recv()
+    ld_mom.wait()
+
+    @pl.loop(0, ROWS // 16)
+    def _(r):
+        at = pl.ds(pl.multiple_of(r * 16, 16), 16)
+        delta = DL[at, :]
+        moment = momentum_coef * M[at, :] + delta
+        M[at, :] = moment
+        GL[at, :] = GL[at, :] - outer_rate * (momentum_coef * moment + delta)
 
     x_parts[1].wait_recv()
     x_parts[2].wait_recv()
@@ -309,13 +317,6 @@
         copy.wait_recv()
     add(slot(1, ZERO), 0, RX, full_pair.at[0], full_pair.at[1])
     last = send(G.at[slot(1, ZERO), gX], x_last, pair)
-
-    keys_swap.wait_recv()
-
-    @pl.loop(0, TOK // 16)
-    def _(r):
-        at = pl.ds(pl.multiple_of(r * 16, 16), 16)
-        o_keys[at, :] = ((acc[at, :] + acc_in[at, :]) * SCALE).astype(bf16)
 
     for copy in fulls[0]:
         copy.wait_recv()

time: 127 us -> 121 us (0.953)
  Pallas kernels: 126 us -> 120 us
    pallas_call x1, Pallas kernels: 121 us -> 116 us  [shards(): pl.pallas_call(kernel, out_shape=held, in_specs=[anywhere] * 5, out_specs...]
where the time goes in v3:
time: 121 us
  Pallas kernels  120 us (99%)
    pallas_call x1, Pallas kernels, shards(): pl.pallas_call(kernel, out_shape=held, in_specs=[anywhere] * 5, out_specs...  116 us
    pallas_call x1, Pallas kernels, shards(): pl.pallas_call(finish, out_shape=(jax.ShapeDtypeStruct((TOK, KV), bf16),...  4.92 us

profile of v3, /device:TPU:0, one launch (start us, length us, event | category | flops | bytes accessed | tf_op | source)
XLA Modules:
  0.0 121.1 jit_solution(10049745523837627322)
XLA Ops:
  0.6 115.5 %step.1 = (bf16[384,1024]{1,0:T(8,128)(2,1)S(1)}, bf16[384,8192]{1,0:T(8,128)(2,1)S(1)}, f32[512,1024]{1,0:T(8,128)S(1)}, f32[512,1024]{1,0:T(8,128)S(1)}, f32[5...) custom-call(bf16[384,8192]{1,0:T(8,128)(2,1)} %hid.1, ...), custom_call_target="tpu_custom_call" | custom-call | flops 19327352832 | bytes 27262976 | tf_op jit(solution)/shard_map/step/pallas_call | solution.py:386
  116.2 4.9 %finish.1 = (bf16[384,1024]{1,0:T(8,128)(2,1)}, bf16[384,8192]{1,0:T(8,128)(2,1)}, f32[512,1024]{1,0:T(8,128)}, f32[512,1024]{1,0:T(8,128)}, f32[512,1024]{1,0:T(8,128)}) custom-call(bf16[384,1024]{1,0:T(8,128)(2,1)S(1)} %get-tuple-element.20.keys, bf16[384,8192]{1,0:T(8,128)(2,1)S(1)} %get-tuple-element.21.back, f32[512,1024]{1,0:T(8,128)S(1)} %get-tuple-element.22.L, ...), custom_call_target="tpu_custom_call" | custom-call | tf_op jit(solution)/shard_map/finish/pallas_call | solution.py:419

commit v4 on v3

--- a/solution.py
+++ b/solution.py
@@ -17,7 +17,7 @@
 inner_rate = 0.3
 mix_weight = 0.5
 
-AX = 304
+AX = 320
 RX = 288
 ZERO, PLUS, MINUS, FAR = 0, 1, 2, 3
 

time: 121 us -> 123 us (1.017)
  Pallas kernels: 120 us -> 122 us
    pallas_call x1, Pallas kernels: 116 us -> 117 us  [shards(): pl.pallas_call(kernel, out_shape=held, in_specs=[anywhere] * 5, out_specs...]
where the time goes in v4:
time: 123 us
  Pallas kernels  122 us (99%)
    pallas_call x1, Pallas kernels, shards(): pl.pallas_call(kernel, out_shape=held, in_specs=[anywhere] * 5, out_specs...  117 us
    pallas_call x1, Pallas kernels, shards(): pl.pallas_call(finish, out_shape=(jax.ShapeDtypeStruct((TOK, KV), bf16),...  4.92 us

profile of v4, /device:TPU:0, one launch (start us, length us, event | category | flops | bytes accessed | tf_op | source)
XLA Modules:
  0.0 122.5 jit_solution(6853249501168315247)
XLA Ops:
  0.6 116.9 %step.1 = (bf16[384,1024]{1,0:T(8,128)(2,1)S(1)}, bf16[384,8192]{1,0:T(8,128)(2,1)S(1)}, f32[512,1024]{1,0:T(8,128)S(1)}, f32[512,1024]{1,0:T(8,128)S(1)}, f32[5...) custom-call(bf16[384,8192]{1,0:T(8,128)(2,1)} %hid.1, ...), custom_call_target="tpu_custom_call" | custom-call | flops 19327352832 | bytes 27262976 | tf_op jit(solution)/shard_map/step/pallas_call | solution.py:386
  117.6 4.9 %finish.1 = (bf16[384,1024]{1,0:T(8,128)(2,1)}, bf16[384,8192]{1,0:T(8,128)(2,1)}, f32[512,1024]{1,0:T(8,128)}, f32[512,1024]{1,0:T(8,128)}, f32[512,1024]{1,0:T(8,128)}) custom-call(bf16[384,1024]{1,0:T(8,128)(2,1)S(1)} %get-tuple-element.20.keys, bf16[384,8192]{1,0:T(8,128)(2,1)S(1)} %get-tuple-element.21.back, f32[512,1024]{1,0:T(8,128)S(1)} %get-tuple-element.22.L, ...), custom_call_target="tpu_custom_call" | custom-call | tf_op jit(solution)/shard_map/finish/pallas_call | solution.py:419
